TPU v7x, 32 devices: a whole 2x2x4 slice. The times are simulated.
32 devices in a mesh: frames: 16 (over z, y, core), tblk: 2 (over x).
Axes of the slice: x: 2, y: 2, z: 4, core: 2. Of those that a mesh axis runs over, the one named last changes fastest.
Arguments:
- momentum: bfloat16 [2, 16, 3, 128, 128, 128], P('tblk', 'frames'), may hold values from -6 to 6
- mode_list: int32 [2048], replicated, may hold values from 2113 to 137312, as said below
Outputs:
- correlation: float32 [2, 16, 2048], P('tblk', None, 'frames')
- strength: float32 [2, 2048], P('tblk', 'frames')
Inputs may be any that keep to these rules, and one draw needn't show every extreme that they name: `mode_list`: distinct encodings (kz * 65 + ky + 32) * 65 + kx + 32 of integer wavevectors with kx^2 + ky^2 + kz^2 <= 32^2 in the upper half space (kz > 0, or kz = 0 and ky > 0, or kz = ky = 0 and kx > 0). Owner o along frames owns entries o * 128 to (o + 1) * 128 - 1.
All inputs are finite; a program needn't handle non-finite values.
Results may differ from a plain program's by a relative error of at most 0.0012.
Values sent between devices are 32-bit elements; how exact they have to be, the bound alone decides.
A program may use at most 192 MiB of HBM per device.

v0:
```python
import math

import jax
import jax.numpy as jnp
from jax import lax
from jax.sharding import PartitionSpec as P

KMAX = 32
LAG_MAX = 64


highest = lax.Precision.HIGHEST


def passed_along(value, axis, steps):
    count = lax.axis_size(axis)
    first, last = (max(0, -steps), min(count, count - steps))
    return lax.ppermute(value, axis, [(source, source + steps) for source in range(first, last)])


def tables(length, lowest, topmost):
    position = jnp.arange(length, dtype=jnp.int32)
    frequency = jnp.arange(lowest, topmost + 1, dtype=jnp.int32)
    turn_count = jnp.mod(position[:, None] * frequency[None, :], length).astype(jnp.float32)
    angles = turn_count * (2.0 * math.pi / length)
    return (jnp.cos(angles), jnp.sin(angles))


def contract_last(table, matrix, exact):
    if exact:
        return lax.dot_general(
            table,
            matrix,
            (((1,), (1,)), ((), ())),
            precision=highest,
            preferred_element_type=jnp.float32,
        )
    return lax.dot_general(
        table, matrix, (((1,), (1,)), ((), ())), preferred_element_type=jnp.float32
    )


def wave_vectors(mode_list):
    side_len = 2 * KMAX + 1
    z_freq = mode_list // (side_len * side_len)
    y_freq = mode_list // side_len % side_len - KMAX
    x_freq = mode_list % side_len - KMAX
    return jnp.stack([x_freq, y_freq, z_freq]).astype(jnp.float32)


def on_device(momentum, mode_list):
    frame_data = momentum[0, 0]
    grid_len = frame_data.shape[-1]
    side_len = 2 * KMAX + 1
    half_len = KMAX + 1
    cos_z, sin_z = tables(grid_len, 0, KMAX)
    table_z = jnp.concatenate([cos_z, -sin_z], axis=1).T.astype(jnp.bfloat16)
    half_z = contract_last(table_z, frame_data.reshape(3 * grid_len * grid_len, grid_len), False)
    stacked = half_z.reshape(2 * half_len * 3 * grid_len, grid_len)
    cos_w, sin_w = tables(grid_len, -KMAX, KMAX)
    table_w = jnp.concatenate([cos_w.T, sin_w.T], axis=0)
    along_y = contract_last(table_w, stacked, True)
    block_width = half_len * 3 * grid_len
    real_y = along_y[:side_len, :block_width] + along_y[side_len:, block_width:]
    imag_y = along_y[:side_len, block_width:] - along_y[side_len:, :block_width]
    stacked_x = jnp.concatenate([real_y, imag_y], axis=0).reshape(
        2 * side_len * half_len * 3, grid_len
    )
    along_x = contract_last(table_w, stacked_x, True)
    block_width = side_len * half_len * 3
    real_x = along_x[:side_len, :block_width] + along_x[side_len:, block_width:]
    imag_x = along_x[:side_len, block_width:] - along_x[side_len:, :block_width]
    spectrum = jnp.stack([real_x, imag_x]).reshape(2, side_len * side_len * half_len, 3)
    spectrum = spectrum.transpose(0, 2, 1).reshape(
        6, side_len * side_len * half_len
    ) * grid_len ** (-1.5)
    z_freq = mode_list // (side_len * side_len)
    y_index = mode_list // side_len % side_len
    x_index = mode_list % side_len
    position = (x_index * side_len + y_index) * half_len + z_freq
    current = jnp.take(spectrum, position, axis=1)
    real_part = current[:3]
    imag_part = current[3:]
    wave_vec = wave_vectors(mode_list)
    wave_sq = jnp.sum(wave_vec * wave_vec, axis=0)
    x_comp = wave_vec[0]
    y_comp = wave_vec[1]
    z_comp = wave_vec[2]
    magnitude = jnp.abs(wave_vec)
    pick_x = (magnitude[0] <= magnitude[1]) & (magnitude[0] <= magnitude[2])
    pick_y = jnp.logical_not(pick_x) & (magnitude[1] <= magnitude[2])
    zeros_row = jnp.zeros_like(x_comp)
    first_axis = jnp.stack(
        [
            jnp.where(pick_x, zeros_row, jnp.where(pick_y, -z_comp, y_comp)),
            jnp.where(pick_x, z_comp, jnp.where(pick_y, zeros_row, -x_comp)),
            jnp.where(pick_x, -y_comp, jnp.where(pick_y, x_comp, zeros_row)),
        ]
    )
    first_axis = first_axis / jnp.sqrt(jnp.sum(first_axis * first_axis, axis=0, keepdims=True))
    second_axis = jnp.cross(wave_vec, first_axis, axis=0) / jnp.sqrt(wave_sq)[None]
    channels = jnp.stack(
        [
            jnp.sum(first_axis * real_part, axis=0),
            jnp.sum(second_axis * real_part, axis=0),
            jnp.sum(first_axis * imag_part, axis=0),
            jnp.sum(second_axis * imag_part, axis=0),
        ]
    )
    chan_count = channels.shape[0]
    owners = lax.axis_size("frames")
    per_owner = mode_list.shape[0] // owners
    packet = channels.reshape(1, chan_count, owners, per_owner)
    lag_len = min(LAG_MAX, owners)
    is_last = lax.axis_index("tblk") == lax.axis_size("tblk") - 1
    modes_here = lax.all_to_all(packet, "frames", split_axis=2, concat_axis=0, tiled=True)[
        :, :, 0, :
    ]
    item_count = modes_here.shape[2]
    tail_rows = modes_here[: lag_len - 1]
    later_frames = passed_along(tail_rows, "tblk", -1)
    extended = jnp.concatenate(
        [modes_here, later_frames, jnp.zeros((1, chan_count, item_count), jnp.float32)], axis=0
    )
    lag_sums = jnp.zeros((item_count, lag_len), jnp.float32)
    for tile_index in range(owners // lag_len):
        tile_start = tile_index * lag_len
        anchor = modes_here[tile_start : tile_start + lag_len]
        partner = extended[tile_start : tile_start + 2 * lag_len]
        outer_prod = jnp.einsum("acm,scm->mas", anchor, partner, precision=highest)
        flat_prod = outer_prod.reshape(item_count, 2 * lag_len * lag_len)
        flat_prod = jnp.pad(flat_prod, ((0, 0), (0, lag_len)))
        diagonal = flat_prod.reshape(item_count, lag_len, 2 * lag_len + 1)[:, :, :lag_len]
        lag_sums = lag_sums + jnp.sum(diagonal, axis=1)
    lag_values = jnp.arange(lag_len, dtype=jnp.float32)
    pair_count = jnp.where(is_last, owners - lag_values, jnp.float32(owners))
    lagged = lag_sums.T / pair_count[:, None]
    strength = lagged[0:1]
    correlation, strength = (lagged / (strength + 1e-06), strength)
    return (correlation[None], strength)


def solution(mesh):
    placed = (P("tblk", "frames", None, None, None, None), P())
    return jax.shard_map(
        on_device,
        mesh=mesh,
        in_specs=placed,
        out_specs=(P("tblk", None, "frames"), P("tblk", "frames")),
        check_vma=False,
    )
```

profile of v0, /device:TPU:0, one launch (start us, length us, event | category | flops | bytes accessed | tf_op | source)
XLA Modules:
  0.0 352.0 jit_solution(17502970790321785365)
XLA Ops:
  0.6 0.1 negate_convert_fusion
  0.7 1.3 compare_and_fusion.2
  2.1 0.7 fusion.30
  2.8 1.2 multiply_reduce_fusion.3
  4.0 0.7 fusion.35
  4.7 17.3 %fusion.21 = f32[66,49152]{1,0:T(8,128)} fusion(bf16[49152,128]{1,0:T(8,128)(2,1)} %bitcast.44, bf16[128,33]{0,1:T(8,128)(2,1)S(1)} %get-tuple-element.32, bf16[128,33]{0,1:T(8,128)(2,1)S(1)} %get-tuple-element.33), kind=kOutput, calls=%fused_computation.53 | convolution fusion | flops 830505984 | bytes 25575936 | tf_op jit(solution)/shard_map/dot_general | solution.py:38
  22.0 13.9 %reshape.176 = f32[25344,128]{1,0:T(8,128)} reshape(f32[66,49152]{1,0:T(8,128)} %fusion.21) | data formatting | bytes 25952256 | tf_op jit(solution)/shard_map/reshape | solution.py:59
  35.9 0.2 fusion.26
  36.1 17.8 %fusion.8 = f32[130,25344]{1,0:T(8,128)} fusion(f32[25344,128]{1,0:T(8,128)} %reshape.176, f32[65,128]{1,0:T(8,128)S(1)} %get-tuple-element.31, f32[65,128]{1,0:T(8,128)S(1)} %get-tuple-element.30), kind=kOutput, calls=%fused_computation.22 | convolution fusion | flops 5060706304 | bytes 26221568 | tf_op jit(solution)/shard_map/dot_general | solution.py:31
  53.9 5.9 %slice_add_fusion = (f32[65,12672]{1,0:T(8,128)S(1)}, f32[65,12672]{1,0:T(8,128)S(1)}) fusion(f32[130,25344]{1,0:T(8,128)} %fusion.8), kind=kLoop, calls=%fused_computation.3 | loop fusion | flops 1647360 | bytes 19768320 | tf_op jit(solution)/shard_map/add | solution.py:64
  59.9 3.3 pad_maximum_fusion
  63.1 7.3 %reshape.177 = f32[12870,128]{1,0:T(8,128)} reshape(f32[130,12672]{1,0:T(8,128)} %pad_maximum_fusion) | data formatting | bytes 13178880 | tf_op jit(solution)/shard_map/reshape | solution.py:66
  70.5 9.1 %fusion.7 = f32[130,12870]{1,0:T(8,128)S(1)} fusion(f32[12870,128]{1,0:T(8,128)} %reshape.177, f32[65,128]{1,0:T(8,128)S(1)} %get-tuple-element.31, f32[65,128]{1,0:T(8,128)S(1)} %get-tuple-element.30), kind=kOutput, calls=%fused_computation.21 | convolution fusion | flops 2569898240 | bytes 13348400 | tf_op jit(solution)/shard_map/dot_general | solution.py:31
  79.5 2.3 slice_add_fusion.1
  81.8 56.1 %stack.48 = f32[1,139425,3]{2,1,0:T(8,128)} reshape(f32[65,6435]{1,0:T(8,128)} %get-tuple-element.17) | data formatting | bytes 3346200 | tf_op jit(solution)/shard_map/stack | solution.py:73
  137.9 37.7 %copy.63 = f32[1,139425,3]{1,0,2:T(1,128)S(1)} copy(f32[1,139425,3]{2,1,0:T(8,128)} %stack.48) | data formatting | bytes 3346200 | tf_op jit(solution)/shard_map/stack | solution.py:73
  175.6 42.6 %stack.47 = f32[1,139425,3]{2,1,0:T(8,128)} reshape(f32[65,6435]{1,0:T(8,128)S(1)} %get-tuple-element.16) | data formatting | bytes 3346200 | tf_op jit(solution)/shard_map/stack | solution.py:73
  218.2 37.7 %copy.62 = f32[1,139425,3]{1,0,2:T(1,128)S(1)} copy(f32[1,139425,3]{2,1,0:T(8,128)} %stack.47) | data formatting | bytes 3346200 | tf_op jit(solution)/shard_map/stack | solution.py:73
  255.9 4.4 %fusion = f32[2,3,139425]{2,0,1:T(2,128)S(1)} fusion(f32[1,139425,3]{1,0,2:T(1,128)S(1)} %copy.63, f32[1,139425,3]{1,0,2:T(1,128)S(1)} %copy.62), kind=kLoop, calls=%fused_computation.5 | loop fusion | flops 1673100 | bytes 6692400 | tf_op jit(solution)/shard_map/mul | solution.py:74
  260.3 3.0 copy.64
  263.3 5.8 %mul.187 = f32[6,139425]{1,0:T(8,128)} reshape(f32[2,3,139425]{2,1,0:T(4,128)} %copy.64) | data formatting | bytes 6692400 | tf_op jit(solution)/shard_map/mul | solution.py:74
  269.2 0.0 copy-start.3
  269.2 0.0 copy-start.4
  269.2 0.0 copy-start.5
  269.2 0.0 copy-start.2
  269.2 32.6 %copy.65 = f32[6,139425]{0,1:T(8,128)} copy(f32[6,139425]{1,0:T(8,128)} %mul.187) | data formatting | bytes 6692400 | tf_op jit(solution)/shard_map/mul | solution.py:74
  301.8 0.0 copy-done.3
  301.8 20.7 %gather_fusion = f32[2048,6]{1,0:T(8,128)S(1)} fusion(f32[6,139425]{0,1:T(8,128)} %copy.65, s32[2048]{0:T(1024)S(1)} %broadcast_clamp_fusion), kind=kCustom, calls=%fused_computation | custom fusion | bytes 106496 | tf_op jit(solution)/shard_map/jit(_take)/gather | solution.py:81
  322.5 0.3 copy.66
  322.8 0.0 copy-done.4
  322.8 0.0 copy-done
  322.9 0.0 copy-done.1
  322.9 0.1 select_select_fusion.2
  322.9 0.1 select_select_fusion.1
  323.1 0.0 copy-done.5
  323.1 0.0 copy-done.2
  323.2 0.1 multiply_reduce_fusion.4
  323.3 0.6 copy.67
  324.0 7.4 %all-to-all-start = ((f32[1,4,16,128]{3,1,0,2:T(4,128)}), f32[1,4,16,128]{3,1,0,2:T(4,128)S(1)}, u32[]{:S(2)}, u32[]{:S(2)}) async-start(f32[1,4,16,128]{3,1,0,2:T(4,128)} %copy.67), calls=%async_computation | async-start | bytes 65536 | tf_op jit(solution)/shard_map/all_to_all | solution.py:116
  331.4 6.6 %all-to-all-done = f32[1,4,16,128]{3,1,0,2:T(4,128)S(1)} async-done(((f32[1,4,16,128]{3,1,0,2:T(4,128)}), f32[1,4,16,128]{3,1,0,2:T(4,128)S(1)}, u32[]{:S(2)}, u32[]{:S(2)}) %all-to-all-start) | async-done | bytes 32800 | tf_op jit(solution)/shard_map/all_to_all | solution.py:116
  338.0 0.2 copy.68
  338.2 1.3 collective-permute-start
  339.5 0.1 pad.7.clone
  339.6 8.4 %collective-permute-done = f32[15,4,128]{0,1,2:T(4,128)S(1)} collective-permute-done((f32[15,4,128]{0,1,2:T(4,128)S(1)}, f32[15,4,128]{0,1,2:T(4,128)S(1)}, u32[]{:S(2)}, u32[]{:S(2)}) %collective-permute-start) | collective-permute-done | bytes 30752 | tf_op jit(solution)/shard_map/ppermute | solution.py:18
  348.0 2.0 fusion.1
  350.0 0.4 copy.69
  350.5 0.6 add_bitcast_fusion
  351.1 0.7 divide_bitcast_fusion
  (16 shorter events, 0.3 us)
Async XLA Ops:
  269.2 32.6 %copy-start.3 = (s32[2048]{0:T(1024)S(1)}, s32[2048]{0:T(1024)}, u32[]{:S(2)}) copy-start(s32[2048]{0:T(1024)} %get-tuple-element.11) | copy-start | bytes 24580
  269.2 53.6 %copy-start.4 = (f32[2048]{0:T(1024)S(1)}, f32[2048]{0:T(1024)}, u32[]{:S(2)}) copy-start(f32[2048]{0:T(1024)} %get-tuple-element.25) | copy-start | bytes 24580
  269.2 53.7 %copy-start = (f32[3,2048]{1,0:T(4,128)S(1)}, f32[3,2048]{1,0:T(4,128)}, u32[]{:S(2)}) copy-start(f32[3,2048]{1,0:T(4,128)} %get-tuple-element.26) | copy-start | bytes 73732
  269.2 53.7 %copy-start.1 = (f32[3,2048]{1,0:T(4,128)S(1)}, f32[3,2048]{1,0:T(4,128)}, u32[]{:S(2)}) copy-start(f32[3,2048]{1,0:T(4,128)} %get-tuple-element.24) | copy-start | bytes 73732
  269.2 53.9 %copy-start.5 = (pred[2048]{0:T(1024)(128)(4,1)S(1)}, pred[2048]{0:T(1024)(128)(4,1)}, u32[]{:S(2)}) copy-start(pred[2048]{0:T(1024)(128)(4,1)} %get-tuple-element.10) | copy-start | bytes 6148
  269.2 53.9 %copy-start.2 = (f32[2048,3]{0,1:T(4,128)S(1)}, f32[2048,3]{0,1:T(4,128)}, u32[]{:S(2)}) copy-start(f32[2048,3]{0,1:T(4,128)} %get-tuple-element.23) | copy-start | bytes 73732
  324.0 14.0 %all-to-all-start = ((f32[1,4,16,128]{3,1,0,2:T(4,128)}), f32[1,4,16,128]{3,1,0,2:T(4,128)S(1)}, u32[]{:S(2)}, u32[]{:S(2)}) async-start(f32[1,4,16,128]{3,1,0,2:T(4,128)} %copy.67), calls=%async_computation | async-start | bytes 65536 | tf_op jit(solution)/shard_map/all_to_all | solution.py:116
  338.2 9.8 %collective-permute-start = (f32[15,4,128]{0,1,2:T(4,128)S(1)}, f32[15,4,128]{0,1,2:T(4,128)S(1)}, u32[]{:S(2)}, u32[]{:S(2)}) collective-permute-start(f32[15,4,128]{0,1,2:T(4,128)S(1)} %slice_bitcast_fusion), channel_id=1, source_target_pairs={{1,0},{3,2},{5,4},{7,6},{9,8},{11,10},{13,12},{15,14},{17,16},{19,... | collective-permute-start | bytes 92168 | tf_op jit(solution)/shard_map/ppermute | solution.py:18
where the time goes:
time: 358 us; the launch traced here: 352 us
  local copies, waits for them, and re-layouts  259 us (72%)
  matrix products  46.2 us (13%)
  other arithmetic  21.8 us (6%)
  waiting for transfers between devices  15 us (4%)
  starting transfers between devices  8.68 us (2%)
    another operation x4, local copies, waits for them, and re-layouts, on_device(): jnp.stack([real_x, imag_x]).reshape(2, side_len * side_len * half_len, 3)  174 us
    mul x3, local copies, waits for them, and re-layouts, on_device(): spectrum.transpose(0, 2, 1).reshape(6, side_len * side_len * half_len)  41.5 us
    dot_general x2, matrix products, contract_last(): lax.dot_general(table, matrix, (((1,), (1,)), ((), ())), precision=highes...  26.9 us
    gather x2, local copies, waits for them, and re-layouts, on_device(): current = jnp.take(spectrum, position, axis=1)  21 us
    dot_general x1, matrix products, contract_last(): lax.dot_general(table, matrix, (((1,), (1,)), ((), ())), preferred_elemen...  17.3 us
    reshape x1, local copies, waits for them, and re-layouts, on_device(): stacked = half_z.reshape(2 * half_len * 3 * grid_len, grid_len)  13.9 us
    ppermute x1, waiting for transfers between devices, passed_along(): lax.ppermute(value, axis, [(source, source + steps) for source in range(f...  8.4 us
    all_to_all x1, starting transfers between devices, on_device(): lax.all_to_all(packet, 'frames', split_axis=2, concat_axis=0, tiled=True)  7.39 us
  transfers between devices with their start and end apart: 2, of which 2 were waited for; matrix products, arithmetic and copies ran while one was open for 0% of the time, Pallas kernels for 0%

commit v1 on v0

v1 whole, which is shorter than its diff:
```python
import functools

import jax
import jax.numpy as jnp
import ml_dtypes
import numpy as np
from jax import lax
from jax.experimental import pallas as pl
from jax.experimental.pallas import tpu as pltpu
from jax.sharding import PartitionSpec as P

KMAX = 32
LAG_MAX = 64
HALF = KMAX + 1
SIDE = 2 * KMAX + 1
PITCH = -(-HALF // 4) * 4
ROWS = -(-SIDE // 8) * 8
CHANNELS = 8
LANES = 128
LANE_BITS = 7

f32 = jnp.float32
bf16 = jnp.bfloat16
MESH = pl.DeviceIdType.MESH


def split_table(table):
    high = table.astype(np.float32).astype(ml_dtypes.bfloat16)
    low = (table - high.astype(np.float64)).astype(np.float32).astype(ml_dtypes.bfloat16)
    return high, low


def angles(length, frequency):
    turns = np.mod(np.outer(frequency, np.arange(length)), length)
    return turns * (2.0 * np.pi / length)


def y_table(length):
    theta = angles(length, np.arange(HALF))
    table = np.zeros((2 * PITCH, length))
    table[:HALF] = np.cos(theta)
    table[PITCH : PITCH + HALF] = np.sin(theta)
    return np.concatenate(split_table(table), axis=1)


def x_table(length):
    theta = angles(length, np.arange(-KMAX, KMAX + 1))
    table = np.zeros((2 * ROWS, 2 * length))
    table[:SIDE, :length] = np.cos(theta)
    table[:SIDE, length:] = -np.sin(theta)
    table[ROWS : ROWS + SIDE, :length] = -np.sin(theta)
    table[ROWS : ROWS + SIDE, length:] = -np.cos(theta)
    return split_table(table)


def z_table(length):
    theta = angles(length, np.arange(-KMAX, KMAX + 1))
    cos_z = np.cos(theta).astype(np.float32).astype(ml_dtypes.bfloat16).astype(np.float32)
    sin_z = (-np.sin(theta)).astype(np.float32).astype(ml_dtypes.bfloat16).astype(np.float32)
    half = CHANNELS // 2
    return np.stack([cos_z] * CHANNELS + [-sin_z] * half + [sin_z] * half, axis=1)


def decode(mode_list):
    entry = mode_list.astype(f32)
    z_freq = jnp.floor((entry + 0.5) * f32(1.0 / (SIDE * SIDE)))
    rest = entry - z_freq * f32(SIDE * SIDE)
    y_index = jnp.floor((rest + 0.5) * f32(1.0 / SIDE))
    x_freq = rest - y_index * f32(SIDE) - f32(KMAX)
    return x_freq, y_index - f32(KMAX), z_freq


def modes_kernel(
    data_hbm, list_ref, ty_ref, txh_ref, txl_ref, tz_ref, out_ref,
    data, along_y, plane, index_vmem, index_smem, data_sem, index_sem,
):
    comps, grid_len, _, _ = data_hbm.shape
    owners = list_ref.shape[0]
    chunk = 16
    chunks = grid_len // chunk

    def fetch(comp, part):
        rows = pl.ds(part * chunk, chunk)
        return pltpu.make_async_copy(
            data_hbm.at[comp, rows], data.at[comp, rows], data_sem.at[comp, part]
        )

    for comp in range(comps):
        for part in range(chunks):
            fetch(comp, part).start()

    x_freq, y_freq, z_freq = decode(list_ref[...])
    sign = jnp.where(y_freq < 0, f32(-1), f32(1))
    pair = sign * y_freq * f32(ROWS) + sign * x_freq + f32(KMAX)
    index_vmem[...] = (pair * f32(LANES) + sign * z_freq + f32(KMAX)).astype(jnp.int32)
    to_smem = pltpu.make_async_copy(index_vmem, index_smem, index_sem)
    to_smem.start()

    table_y = ty_ref[...]
    table_xh = txh_ref[...]
    table_xl = txl_ref[...]
    for comp in range(comps):

        @pl.loop(0, chunks)
        def _(part):
            fetch(comp, part).wait()
            for step in range(0, chunk, 2):
                x_at = part * chunk + step
                both = jnp.concatenate([data[comp, x_at], data[comp, x_at + 1]], axis=1)
                res = jnp.dot(
                    table_y, jnp.concatenate([both, both], axis=0), preferred_element_type=f32
                )
                first = pl.multiple_of(x_at * 2 * PITCH, 8)
                along_y[pl.ds(first, 2 * PITCH), :] = res[:, :LANES]
                second = pl.multiple_of((x_at + 1) * 2 * PITCH, 8)
                along_y[pl.ds(second, 2 * PITCH), :] = res[:, LANES:]

        @pl.loop(0, (HALF + 1) // 2)
        def _(pair_at):
            ky = pair_at * 2

            def take(row):
                return along_y[pl.ds(row, grid_len, stride=2 * PITCH), :]

            cos_part = jnp.concatenate([take(ky), take(ky + 1)], axis=1)
            sin_part = jnp.concatenate([take(PITCH + ky), take(PITCH + ky + 1)], axis=1)
            block = jnp.concatenate([cos_part, sin_part], axis=0)
            high = block.astype(bf16)
            low = (block - high.astype(f32)).astype(bf16)
            res = jnp.dot(table_xh, high, preferred_element_type=f32)
            res = res + jnp.dot(table_xl, high, preferred_element_type=f32)
            res = res + jnp.dot(table_xh, low, preferred_element_type=f32)
            for which in range(2):
                lanes = slice(which * LANES, (which + 1) * LANES)
                base = (ky + which) * ROWS * CHANNELS + comp
                plane[pl.ds(base, ROWS, stride=CHANNELS), :] = res[:ROWS, lanes]
                plane[pl.ds(base + CHANNELS // 2, ROWS, stride=CHANNELS), :] = res[ROWS:, lanes]

    to_smem.wait()
    lane = lax.broadcasted_iota(jnp.int32, (CHANNELS, LANES), 1)
    row = lax.broadcasted_iota(jnp.int32, (CHANNELS, LANES), 0)
    bits = [1 << level for level in range(LANE_BITS)]
    odd = [(lane & bit) != 0 for bit in bits]
    upper = row < CHANNELS // 2
    scale = f32(float(grid_len) ** -1.5)

    @pl.loop(0, owners)
    def _(owner):
        def leaf(mode):
            code = index_smem[owner, mode]
            pair_at = pl.multiple_of((code >> LANE_BITS) * CHANNELS, CHANNELS)
            freq = code & (LANES - 1)
            value = plane[pl.ds(pair_at, CHANNELS), :]
            swapped = pltpu.roll(value, CHANNELS // 2, 0)
            return value * tz_ref[freq, :CHANNELS] + swapped * tz_ref[freq, CHANNELS:]

        def tree(start, level):
            if level < 0:
                return leaf(start)
            left = tree(start, level - 1)
            right = tree(start + bits[level], level - 1)
            kept = jnp.where(odd[level], right, left)
            moved = jnp.where(odd[level], left, right)
            return kept + pltpu.roll(moved, bits[level], 1)

        total = tree(0, len(bits) - 1)
        current = jnp.where((row & 3) == 3, f32(0), total) * scale
        x_f, y_f, z_f = decode(list_ref[pl.ds(owner, 1), :])
        wave = jnp.where((row & 3) == 0, x_f, jnp.where((row & 3) == 1, y_f, z_f))
        wave_sq = x_f * x_f + y_f * y_f + z_f * z_f
        along = current * wave
        real_dot = jnp.sum(jnp.where(upper, along, f32(0)), axis=0, keepdims=True)
        imag_dot = jnp.sum(jnp.where(upper, f32(0), along), axis=0, keepdims=True)
        removed = wave * (jnp.where(upper, real_dot, imag_dot) / wave_sq)
        out_ref[owner] = current - jnp.where((row & 3) == 3, f32(0), removed)


def frame_modes(frame, mode_rows):
    comps, grid_len = frame.shape[:2]
    owners = mode_rows.shape[0]
    table_xh, table_xl = x_table(grid_len)
    vmem = pl.BlockSpec(memory_space=pltpu.VMEM)
    chunks = grid_len // 16
    return pl.pallas_call(
        modes_kernel,
        out_shape=jax.ShapeDtypeStruct((owners, CHANNELS, LANES), f32),
        in_specs=[pl.BlockSpec(memory_space=pl.ANY)] + [vmem] * 5,
        out_specs=vmem,
        scratch_shapes=[
            pltpu.VMEM(frame.shape, bf16),
            pltpu.VMEM((grid_len * 2 * PITCH, LANES), f32),
            pltpu.VMEM(((HALF + 1) * ROWS * CHANNELS, LANES), f32),
            pltpu.VMEM((owners, LANES), jnp.int32),
            pltpu.SMEM((owners, LANES), jnp.int32),
            pltpu.SemaphoreType.DMA((comps, chunks)),
            pltpu.SemaphoreType.DMA,
        ],
        compiler_params=pltpu.CompilerParams(vmem_limit_bytes=48 * 1024 * 1024),
        name="frame_modes",
    )(
        frame,
        mode_rows,
        jnp.asarray(y_table(grid_len)),
        jnp.asarray(table_xh),
        jnp.asarray(table_xl),
        jnp.asarray(z_table(grid_len)),
    )


def lag_kernel(frames, blocks, lags, packet, corr_ref, strength_ref, held, send_sem, late_sem, recv_sem):
    me = lax.axis_index("frames")
    block = lax.axis_index("tblk")
    tail = lags - 1
    has_earlier = block > 0
    has_later = block < blocks - 1
    sends_back = jnp.logical_and(has_earlier, me < tail)
    barrier = pltpu.get_barrier_semaphore()

    def others(action):
        @pl.loop(1, frames)
        def _(step):
            action(lax.rem(me + step, frames))

    def greet(frame, in_block):
        pl.semaphore_signal(
            barrier, inc=1, device_id={"frames": frame, "tblk": in_block}, device_id_type=MESH
        )

    others(lambda frame: greet(frame, block))

    @pl.when(has_later)
    def _():
        @pl.loop(0, min(tail, frames))
        def _(frame):
            greet(frame, block + 1)

    pl.semaphore_wait(barrier, frames - 1 + jnp.where(sends_back, frames, 0))

    def within(owner):
        return pltpu.make_async_remote_copy(
            src_ref=packet.at[owner],
            dst_ref=held.at[me],
            send_sem=send_sem.at[owner],
            recv_sem=recv_sem.at[me],
            device_id={"frames": owner, "tblk": block},
            device_id_type=MESH,
        )

    def backward(owner):
        return pltpu.make_async_remote_copy(
            src_ref=packet.at[owner],
            dst_ref=held.at[frames + me],
            send_sem=late_sem.at[owner],
            recv_sem=recv_sem.at[frames + me],
            device_id={"frames": owner, "tblk": block - 1},
            device_id_type=MESH,
        )

    def arrival(slot):
        return pltpu.make_async_remote_copy(
            src_ref=held.at[slot],
            dst_ref=held.at[slot],
            send_sem=send_sem.at[0],
            recv_sem=recv_sem.at[slot],
            device_id={"frames": me, "tblk": block},
            device_id_type=MESH,
        )

    @pl.when(sends_back)
    def _():
        @pl.loop(0, frames)
        def _(step):
            backward(lax.rem(me + step, frames)).start()

    others(lambda owner: within(owner).start())
    held[me] = packet[me]

    @pl.when(jnp.logical_not(has_later))
    def _():
        held[pl.ds(frames, lags)] = jnp.zeros((lags,) + held.shape[1:], f32)

    others(lambda frame: arrival(frame).wait_recv())

    @pl.when(has_later)
    def _():
        held[frames + tail] = jnp.zeros(held.shape[1:], f32)

        @pl.loop(0, tail)
        def _(frame):
            arrival(frames + frame).wait_recv()

    anchors = held[pl.ds(0, frames)]

    def lagged(tau, missing):
        products = jnp.sum(anchors * held[pl.ds(tau, frames)], axis=0)
        total = jnp.sum(products, axis=0, keepdims=True)
        whole = f32(frames)
        return total / jnp.where(has_later, whole, whole - missing)

    strength = lagged(0, f32(0))
    strength_ref[...] = strength

    @pl.loop(0, lags)
    def _(tau):
        corr_ref[pl.ds(tau, 1), :] = lagged(tau, tau.astype(f32)) / (strength + f32(1e-06))

    others(lambda owner: within(owner).wait_send())

    @pl.when(sends_back)
    def _():
        @pl.loop(0, frames)
        def _(owner):
            backward(owner).wait_send()


def on_device(momentum, mode_list):
    frame = momentum[0, 0]
    frames = lax.axis_size("frames")
    blocks = lax.axis_size("tblk")
    lags = min(LAG_MAX, frames)
    packet = frame_modes(frame, mode_list.reshape(frames, LANES))
    vmem = pl.BlockSpec(memory_space=pltpu.VMEM)
    correlation, strength = pl.pallas_call(
        functools.partial(lag_kernel, frames, blocks, lags),
        out_shape=(
            jax.ShapeDtypeStruct((lags, LANES), f32),
            jax.ShapeDtypeStruct((1, LANES), f32),
        ),
        in_specs=[vmem],
        out_specs=(vmem, vmem),
        scratch_shapes=[
            pltpu.VMEM((frames + lags, CHANNELS, LANES), f32),
            pltpu.SemaphoreType.DMA((frames,)),
            pltpu.SemaphoreType.DMA((frames,)),
            pltpu.SemaphoreType.DMA((frames + lags,)),
        ],
        compiler_params=pltpu.CompilerParams(collective_id=0, has_side_effects=True),
        name="exchange_and_lags",
    )(packet)
    return correlation[None], strength


def solution(mesh):
    placed = (P("tblk", "frames", None, None, None, None), P())
    return jax.shard_map(
        on_device,
        mesh=mesh,
        in_specs=placed,
        out_specs=(P("tblk", None, "frames"), P("tblk", "frames")),
        check_vma=False,
    )
```

time: 358 us -> 54.9 us (0.15); the launches traced: 352 us -> 54.4 us
  local copies, waits for them, and re-layouts: 259 us -> 7.36 us
  Pallas kernels: 0 us -> 46.4 us
  matrix products: 46.2 us -> 0 us
  other arithmetic: 21.8 us -> 0 us
  waiting for transfers between devices: 15 us -> 0 us
  starting transfers between devices: 8.68 us -> 0 us
    another operation x5 -> x0, local copies, waits for them, and re-layouts: 175 us -> none  [the longest x4 174 us: on_device(): jnp.stack([real_x, imag_x]).reshape(2, side_len * side_len * half_len, 3)]
    pallas_call x0 -> x2, Pallas kernels: none -> 46.4 us  [the longest x1 33.9 us: frame_modes(): pl.pallas_call(modes_kernel, out_shape=jax.ShapeDtypeStruct((owners, CHAN...]
    dot_general x4 -> x0, matrix products: 46.2 us -> none  [the longest x2 26.9 us: contract_last(): lax.dot_general(table, matrix, (((1,), (1,)), ((), ())), precision=highes...]
    mul x3 -> x0, local copies, waits for them, and re-layouts: 41.5 us -> none  [on_device(): spectrum.transpose(0, 2, 1).reshape(6, side_len * side_len * half_len)]
    reshape x3 -> x0, local copies, waits for them, and re-layouts: 21.2 us -> none  [the longest x1 13.9 us: on_device(): stacked = half_z.reshape(2 * half_len * 3 * grid_len, grid_len)]
    gather x2 -> x0, local copies, waits for them, and re-layouts: 21 us -> none  [on_device(): current = jnp.take(spectrum, position, axis=1)]
    ppermute x1 -> x0, waiting for transfers between devices: 8.4 us -> none  [passed_along(): lax.ppermute(value, axis, [(source, source + steps) for source in range(f...]
    add x3 -> x0, other arithmetic: 8.23 us -> none  [the longest x1 5.93 us: on_device(): real_y = along_y[:side_len, :block_width] + along_y[side_len:, block_width:]]
  transfers between devices with their start and end apart: 2 -> 0, of which waited for: 2 -> 0; matrix products, arithmetic and copies ran while one was open for 0% -> 0% of each run, Pallas kernels for 0% -> 0%
where the time goes in v1:
time: 54.9 us; the launch traced here: 54.4 us
  Pallas kernels  46.4 us (85%)
  local copies, waits for them, and re-layouts  7.36 us (13%)
  between operations  0.67 us (1%)
    pallas_call x1, Pallas kernels, frame_modes(): pl.pallas_call(modes_kernel, out_shape=jax.ShapeDtypeStruct((owners, CHAN...  33.9 us
    pallas_call x1, Pallas kernels, on_device(): pl.pallas_call(functools.partial(lag_kernel, frames, blocks, lags), out_s...  12.5 us
    unnamed x14, local copies, waits for them, and re-layouts  7.36 us

profile of v1, /device:TPU:0, one launch (start us, length us, event | category | flops | bytes accessed | tf_op | source)
XLA Modules:
  0.0 54.4 jit_solution(13503828740918330988)
XLA Ops:
  0.6 0.0 copy-start
  0.6 1.0 %copy-done = f32[65,16,128]{2,1,0:T(8,128)S(1)} copy-done((f32[65,16,128]{2,1,0:T(8,128)S(1)}, f32[65,16,128]{2,1,0:T(8,128)}, u32[]{:S(2)}) %copy-start) | copy-done | bytes 532504
  1.7 0.0 copy-start.2
  1.7 0.9 %copy-done.2 = bf16[144,256]{1,0:T(8,128)(2,1)S(1)} copy-done((bf16[144,256]{1,0:T(8,128)(2,1)S(1)}, bf16[144,256]{1,0:T(8,128)(2,1)}, u32[]{:S(2)}) %copy-start.2) | copy-done | bytes 73752
  2.6 0.0 copy-start.3
  2.6 0.9 %copy-done.3 = bf16[144,256]{1,0:T(8,128)(2,1)S(1)} copy-done((bf16[144,256]{1,0:T(8,128)(2,1)S(1)}, bf16[144,256]{1,0:T(8,128)(2,1)}, u32[]{:S(2)}) %copy-start.3) | copy-done | bytes 73752
  3.4 0.0 copy-start.4
  3.4 0.8 %copy-done.4 = bf16[72,256]{1,0:T(8,128)(2,1)S(1)} copy-done((bf16[72,256]{1,0:T(8,128)(2,1)S(1)}, bf16[72,256]{1,0:T(8,128)(2,1)}, u32[]{:S(2)}) %copy-start.4) | copy-done | bytes 36888
  4.2 0.0 copy-start.5
  4.2 0.7 %copy-done.5 = s32[2048]{0:T(1024)S(1)} copy-done((s32[2048]{0:T(1024)S(1)}, s32[2048]{0:T(1024)}, u32[]{:S(2)}) %copy-start.5) | copy-done | bytes 8216
  4.9 33.9 %frame_modes.1.packet = f32[16,8,128]{2,1,0:T(8,128)S(1)} custom-call(bf16[3,128,128,128]{3,2,1,0:T(8,128)(2,1)} %bitcast.4, s32[16,128]{1,0:T(8,128)S(1)} %bitcast.3, bf16[72,256]{1,0:T(8,128)(2,1)S(1)} %copy-done.4, bf16[144,256]{1,0:T(8,128)(2,1)S(1)} %copy-done.3, bf16[144,256]{1,0:T(8,128)(2,1)S(1)} %copy-done.2, f32[65,16,128]{2,1,0:T(8,128)S(1)} %copy-done), custom_call_target="tpu_custom_call" | custom-call | tf_op jit(solution)/shard_map/frame_modes/pallas_call | solution.py:184
  38.8 0.0 copy-start.1
  38.9 0.6 %copy-done.1 = f32[16,8,128]{2,1,0:T(8,128)} copy-done((f32[16,8,128]{2,1,0:T(8,128)}, f32[16,8,128]{2,1,0:T(8,128)S(1)}, u32[]{:S(2)}) %copy-start.1) | copy-done | bytes 65560
  39.5 12.5 %exchange_and_lags.1 = (f32[16,128]{1,0:T(8,128)}, f32[1,128]{1,0:T(1,128)}) custom-call(f32[16,8,128]{2,1,0:T(8,128)} %copy-done.1), custom_call_target="tpu_custom_call" | custom-call | tf_op jit(solution)/shard_map/exchange_and_lags/pallas_call | solution.py:323
  51.9 1.3 %copy.10 = f32[1,16,128]{2,1,0:T(8,128)} copy(f32[1,16,128]{2,1,0:T(8,128)} %bitcast.5) | data formatting | bytes 16384
  53.2 1.2 %copy.11 = f32[1,128]{1,0:T(1,128)} copy(f32[1,128]{1,0:T(1,128)} %get-tuple-element.9) | data formatting | bytes 1024
Async XLA Ops:
  0.6 1.0 %copy-start = (f32[65,16,128]{2,1,0:T(8,128)S(1)}, f32[65,16,128]{2,1,0:T(8,128)}, u32[]{:S(2)}) copy-start(f32[65,16,128]{2,1,0:T(8,128)} %constant.11.clone.tz_ref) | copy-start | bytes 1597444
  1.7 0.9 %copy-start.2 = (bf16[144,256]{1,0:T(8,128)(2,1)S(1)}, bf16[144,256]{1,0:T(8,128)(2,1)}, u32[]{:S(2)}) copy-start(bf16[144,256]{1,0:T(8,128)(2,1)} %constant.10.clone.txl_ref) | copy-start | bytes 221188
  2.6 0.9 %copy-start.3 = (bf16[144,256]{1,0:T(8,128)(2,1)S(1)}, bf16[144,256]{1,0:T(8,128)(2,1)}, u32[]{:S(2)}) copy-start(bf16[144,256]{1,0:T(8,128)(2,1)} %constant.9.clone.txh_ref) | copy-start | bytes 221188
  3.4 0.8 %copy-start.4 = (bf16[72,256]{1,0:T(8,128)(2,1)S(1)}, bf16[72,256]{1,0:T(8,128)(2,1)}, u32[]{:S(2)}) copy-start(bf16[72,256]{1,0:T(8,128)(2,1)} %constant.8.clone.ty_ref) | copy-start | bytes 110596
  4.2 0.7 %copy-start.5 = (s32[2048]{0:T(1024)S(1)}, s32[2048]{0:T(1024)}, u32[]{:S(2)}) copy-start(s32[2048]{0:T(1024)} %param.7) | copy-start | bytes 24580
  38.8 0.6 %copy-start.1 = (f32[16,8,128]{2,1,0:T(8,128)}, f32[16,8,128]{2,1,0:T(8,128)S(1)}, u32[]{:S(2)}) copy-start(f32[16,8,128]{2,1,0:T(8,128)S(1)} %frame_modes.1.packet) | copy-start | bytes 196612

commit v2 on v1

v2 whole, which is shorter than its diff:
```python
import functools

import jax
import jax.numpy as jnp
import ml_dtypes
import numpy as np
from jax import lax
from jax.experimental import pallas as pl
from jax.experimental.pallas import tpu as pltpu
from jax.sharding import PartitionSpec as P

KMAX = 32
LAG_MAX = 64
HALF = KMAX + 1
SIDE = 2 * KMAX + 1
PITCH = -(-HALF // 4) * 4
ROWS = -(-SIDE // 8) * 8
CHANNELS = 8
LANES = 128
LANE_BITS = 7
DIVIDE_BITS = 19

f32 = jnp.float32
bf16 = jnp.bfloat16
MESH = pl.DeviceIdType.MESH


def split_table(table):
    high = table.astype(np.float32).astype(ml_dtypes.bfloat16)
    low = (table - high.astype(np.float64)).astype(np.float32).astype(ml_dtypes.bfloat16)
    return high, low


def angles(length, frequency):
    turns = np.mod(np.outer(frequency, np.arange(length)), length)
    return turns * (2.0 * np.pi / length)


def y_table(length):
    theta = angles(length, np.arange(HALF))
    table = np.zeros((2 * PITCH, length))
    table[:HALF] = np.cos(theta)
    table[PITCH : PITCH + HALF] = np.sin(theta)
    return np.concatenate(split_table(table), axis=0)


def x_table(length):
    theta = angles(length, np.arange(-KMAX, KMAX + 1))
    table = np.zeros((2 * ROWS, 2 * length))
    table[:SIDE, :length] = np.cos(theta)
    table[:SIDE, length:] = -np.sin(theta)
    table[ROWS : ROWS + SIDE, :length] = -np.sin(theta)
    table[ROWS : ROWS + SIDE, length:] = -np.cos(theta)
    both = np.concatenate(split_table(table), axis=0)
    return np.stack([both[:, :length], both[:, length:]])


def z_table(length):
    theta = angles(length, np.arange(-KMAX, KMAX + 1))
    cos_z = np.cos(theta).astype(np.float32).astype(ml_dtypes.bfloat16).astype(np.float32)
    sin_z = (-np.sin(theta)).astype(np.float32).astype(ml_dtypes.bfloat16).astype(np.float32)
    half = CHANNELS // 2
    return np.stack([cos_z] * CHANNELS + [-sin_z] * half + [sin_z] * half, axis=1)


def by_side(value):
    return (value * (-(-(1 << DIVIDE_BITS) // SIDE))) >> DIVIDE_BITS


def decode(mode_list):
    rest = by_side(mode_list)
    z_freq = by_side(rest)
    return mode_list - rest * SIDE - KMAX, rest - z_freq * SIDE - KMAX, z_freq


def program_kernel(
    frames, blocks, lags, frame_hbm, list_hbm, ty_hbm, tx_hbm, tz_hbm, lagged_ref,
    data, mode_rows, ty_ref, tx_ref, tz_ref, along_y, plane, place_vmem, place_smem,
    freq_vmem, freq_smem, packet, held, data_sem, table_sem, place_sem,
    send_sem, late_sem, recv_sem,
):
    comps, grid_len, _, _ = frame_hbm.shape
    chunk = 16
    chunks = grid_len // chunk
    me = lax.axis_index("frames")
    block = lax.axis_index("tblk")
    tail = lags - 1
    has_later = block < blocks - 1
    sends_back = jnp.logical_and(block > 0, me < tail)
    barrier = pltpu.get_barrier_semaphore()

    def fetch(comp, part):
        rows = pl.ds(part * chunk, chunk)
        return pltpu.make_async_copy(
            frame_hbm.at[comp, rows], data.at[comp, rows], data_sem.at[comp, part]
        )

    list_in = pltpu.make_async_copy(list_hbm, mode_rows, table_sem.at[0])
    ty_in = pltpu.make_async_copy(ty_hbm, ty_ref, table_sem.at[1])
    tx_in = pltpu.make_async_copy(tx_hbm, tx_ref, table_sem.at[2])
    tz_in = pltpu.make_async_copy(tz_hbm, tz_ref, table_sem.at[3])
    ty_in.start()
    list_in.start()
    for comp in range(comps):
        for part in range(chunks):
            fetch(comp, part).start()
        if comp == 0:
            tx_in.start()
    tz_in.start()

    def greet(frame, in_block):
        pl.semaphore_signal(
            barrier, inc=1, device_id={"frames": frame, "tblk": in_block}, device_id_type=MESH
        )

    @pl.loop(1, frames)
    def _(step):
        greet(lax.rem(me + step, frames), block)

    @pl.when(has_later)
    def _():
        @pl.loop(0, tail)
        def _(frame):
            greet(frame, block + 1)

    list_in.wait()
    x_freq, y_freq, z_freq = decode(mode_rows[...])
    sign = jnp.where(y_freq < 0, -1, 1)
    place_vmem[...] = sign * (y_freq * ROWS + x_freq) + KMAX
    freq_vmem[...] = sign * z_freq + KMAX
    place_out = pltpu.make_async_copy(place_vmem, place_smem, place_sem.at[0])
    freq_out = pltpu.make_async_copy(freq_vmem, freq_smem, place_sem.at[1])
    place_out.start()
    freq_out.start()

    ty_in.wait()
    table_y = ty_ref[...]
    for comp in range(comps):

        @pl.loop(0, chunks)
        def _(part):
            fetch(comp, part).wait()
            for step in range(0, chunk, 2):
                x_at = part * chunk + step
                both = jnp.concatenate([data[comp, x_at], data[comp, x_at + 1]], axis=1)
                res = jnp.dot(table_y, both, preferred_element_type=f32)
                res = res[: 2 * PITCH] + res[2 * PITCH :]
                first = pl.multiple_of(x_at * 2 * PITCH, 8)
                along_y[pl.ds(first, 2 * PITCH), :] = res[:, :LANES]
                second = pl.multiple_of((x_at + 1) * 2 * PITCH, 8)
                along_y[pl.ds(second, 2 * PITCH), :] = res[:, LANES:]

        if comp == 0:
            tx_in.wait()

        @pl.loop(0, (HALF + 1) // 2)
        def _(pair_at):
            ky = pair_at * 2

            def take(row):
                return along_y[pl.ds(row, grid_len, stride=2 * PITCH), :]

            cos_part = jnp.concatenate([take(ky), take(ky + 1)], axis=1)
            sin_part = jnp.concatenate([take(PITCH + ky), take(PITCH + ky + 1)], axis=1)
            values = jnp.concatenate([cos_part, sin_part], axis=0)
            high = values.astype(bf16)
            low = (values - high.astype(f32)).astype(bf16)
            table_x = jnp.concatenate([tx_ref[0], tx_ref[1]], axis=1)
            res = jnp.dot(table_x, high, preferred_element_type=f32)
            res_low = jnp.dot(table_x[: 2 * ROWS], low, preferred_element_type=f32)
            res = res[: 2 * ROWS] + res[2 * ROWS :] + res_low
            half = CHANNELS // 2
            for which in range(2):
                lanes = slice(which * LANES, (which + 1) * LANES)
                base = (ky + which) * ROWS * 2 * CHANNELS + comp
                real, imag = res[:ROWS, lanes], res[ROWS:, lanes]
                for at, value in enumerate((real, imag, imag, real)):
                    plane[pl.ds(base + at * half, ROWS, stride=2 * CHANNELS), :] = value

    place_out.wait()
    freq_out.wait()
    tz_in.wait()
    pl.semaphore_wait(barrier, frames - 1 + jnp.where(sends_back, frames, 0))

    def within(owner):
        return pltpu.make_async_remote_copy(
            src_ref=packet.at[owner],
            dst_ref=held.at[me],
            send_sem=send_sem.at[owner],
            recv_sem=recv_sem.at[me],
            device_id={"frames": owner, "tblk": block},
            device_id_type=MESH,
        )

    def backward(owner):
        return pltpu.make_async_remote_copy(
            src_ref=packet.at[owner],
            dst_ref=held.at[frames + me],
            send_sem=late_sem.at[owner],
            recv_sem=recv_sem.at[frames + me],
            device_id={"frames": owner, "tblk": block - 1},
            device_id_type=MESH,
        )

    def arrival(slot):
        return pltpu.make_async_remote_copy(
            src_ref=held.at[slot],
            dst_ref=held.at[slot],
            send_sem=send_sem.at[0],
            recv_sem=recv_sem.at[slot],
            device_id={"frames": me, "tblk": block},
            device_id_type=MESH,
        )

    lane = lax.broadcasted_iota(jnp.int32, (CHANNELS, LANES), 1)
    row = lax.broadcasted_iota(jnp.int32, (CHANNELS, LANES), 0)
    bits = [1 << level for level in range(LANE_BITS)]
    odd = [(lane & bit) != 0 for bit in bits]
    upper = row < CHANNELS // 2
    used = (row & 3) != 3
    scale = f32(float(grid_len) ** -1.5)

    @pl.loop(0, frames)
    def _(step):
        owner = lax.rem(me + step, frames)

        def leaf(mode):
            place = place_smem[owner, mode] * (2 * CHANNELS)
            freq = freq_smem[owner, mode]
            value = plane[pl.ds(place, 2 * CHANNELS), :] * tz_ref[freq]
            return value[:CHANNELS] + value[CHANNELS:]

        def tree(start, level):
            if level < 0:
                return leaf(start)
            left = tree(start, level - 1)
            right = tree(start + bits[level], level - 1)
            kept = jnp.where(odd[level], right, left)
            moved = jnp.where(odd[level], left, right)
            return kept + pltpu.roll(moved, bits[level], 1)

        total = tree(0, len(bits) - 1)
        current = jnp.where(used, total, f32(0)) * scale
        x_f, y_f, z_f = (k.astype(f32) for k in decode(mode_rows[pl.ds(owner, 1), :]))
        wave = jnp.where((row & 3) == 0, x_f, jnp.where((row & 3) == 1, y_f, z_f))
        wave_sq = x_f * x_f + y_f * y_f + z_f * z_f
        along = current * wave
        real_dot = jnp.sum(jnp.where(upper, along, f32(0)), axis=0, keepdims=True)
        imag_dot = jnp.sum(jnp.where(upper, f32(0), along), axis=0, keepdims=True)
        removed = wave * (jnp.where(upper, real_dot, imag_dot) / wave_sq)
        transverse = current - jnp.where(used, removed, f32(0))
        packet[owner] = transverse

        @pl.when(sends_back)
        def _():
            backward(owner).start()

        @pl.when(step > 0)
        def _():
            within(owner).start()

        @pl.when(step == 0)
        def _():
            held[me] = transverse

    @pl.when(jnp.logical_not(has_later))
    def _():
        held[pl.ds(frames, lags)] = jnp.zeros((lags,) + held.shape[1:], f32)

    @pl.loop(1, frames)
    def _(step):
        arrival(lax.rem(me + step, frames)).wait_recv()

    @pl.when(has_later)
    def _():
        held[frames + tail] = jnp.zeros(held.shape[1:], f32)

        @pl.loop(0, tail)
        def _(frame):
            arrival(frames + frame).wait_recv()

    anchors = held[pl.ds(0, frames)]

    @pl.loop(0, lags)
    def _(tau):
        products = jnp.sum(anchors * held[pl.ds(tau, frames)], axis=0)
        total = jnp.sum(products, axis=0, keepdims=True)
        whole = f32(frames)
        pairs = jnp.where(has_later, whole, whole - tau.astype(f32))
        lagged_ref[pl.ds(tau, 1), :] = total / pairs

    @pl.loop(1, frames)
    def _(step):
        within(lax.rem(me + step, frames)).wait_send()

    @pl.when(sends_back)
    def _():
        @pl.loop(0, frames)
        def _(owner):
            backward(owner).wait_send()


def on_device(momentum, mode_list):
    frame = momentum[0, 0]
    comps, grid_len = frame.shape[:2]
    frames = lax.axis_size("frames")
    blocks = lax.axis_size("tblk")
    lags = min(LAG_MAX, frames)
    mode_rows = mode_list.reshape(frames, LANES)
    tables = [y_table(grid_len), x_table(grid_len), z_table(grid_len)]
    places = [pltpu.VMEM(mode_rows.shape, jnp.int32), pltpu.SMEM(mode_rows.shape, jnp.int32)]
    lagged = pl.pallas_call(
        functools.partial(program_kernel, frames, blocks, lags),
        out_shape=jax.ShapeDtypeStruct((lags, LANES), f32),
        in_specs=[pl.BlockSpec(memory_space=pl.ANY)] * 5,
        out_specs=pl.BlockSpec(memory_space=pltpu.VMEM),
        scratch_shapes=[pltpu.VMEM(frame.shape, bf16), pltpu.VMEM(mode_rows.shape, jnp.int32)]
        + [pltpu.VMEM(table.shape, table.dtype) for table in tables]
        + [
            pltpu.VMEM((grid_len * 2 * PITCH, LANES), f32),
            pltpu.VMEM(((HALF + 1) * ROWS * 2 * CHANNELS, LANES), f32),
        ]
        + places
        + places
        + [
            pltpu.VMEM((frames, CHANNELS, LANES), f32),
            pltpu.VMEM((frames + lags, CHANNELS, LANES), f32),
            pltpu.SemaphoreType.DMA((comps, grid_len // 16)),
            pltpu.SemaphoreType.DMA((4,)),
            pltpu.SemaphoreType.DMA((2,)),
            pltpu.SemaphoreType.DMA((frames,)),
            pltpu.SemaphoreType.DMA((frames,)),
            pltpu.SemaphoreType.DMA((frames + lags,)),
        ],
        compiler_params=pltpu.CompilerParams(
            collective_id=0, has_side_effects=True, vmem_limit_bytes=56 * 1024 * 1024
        ),
        name="modes_exchange_lags",
    )(frame, mode_rows, *[jnp.asarray(table) for table in tables])
    strength = lagged[0:1]
    return (lagged / (strength + 1e-06))[None], strength


def solution(mesh):
    placed = (P("tblk", "frames", None, None, None, None), P())
    return jax.shard_map(
        on_device,
        mesh=mesh,
        in_specs=placed,
        out_specs=(P("tblk", None, "frames"), P("tblk", "frames")),
        check_vma=False,
    )
```

time: 54.9 us -> 49.1 us (0.89)
  local copies, waits for them, and re-layouts: 7.36 us -> 0 us
  other arithmetic: 0 us -> 2.49 us
  Pallas kernels: 46.4 us -> 45.6 us
    unnamed x14 -> x0, local copies, waits for them, and re-layouts: 7.36 us -> none
    broadcast_in_dim x0 -> x1, other arithmetic: none -> 1.3 us  [on_device(): return ((lagged / (strength + 1e-06))[None], strength)]
    div x0 -> x1, other arithmetic: none -> 1.18 us  [on_device(): return ((lagged / (strength + 1e-06))[None], strength)]
    pallas_call x2 -> x1, Pallas kernels: 46.4 us -> 45.6 us  [on_device(): pl.pallas_call(functools.partial(program_kernel, frames, blocks, lags), o...]
where the time goes in v2:
time: 49.1 us; the launch traced here: 48.7 us
  Pallas kernels  45.6 us (93%)
  other arithmetic  2.49 us (5%)
  between operations  0.64 us (1%)
    pallas_call x1, Pallas kernels, on_device(): pl.pallas_call(functools.partial(program_kernel, frames, blocks, lags), o...  45.6 us
    broadcast_in_dim x1, other arithmetic, on_device(): return ((lagged / (strength + 1e-06))[None], strength)  1.3 us
    div x1, other arithmetic, on_device(): return ((lagged / (strength + 1e-06))[None], strength)  1.18 us

profile of v2, /device:TPU:0, one launch (start us, length us, event | category | flops | bytes accessed | tf_op | source)
XLA Modules:
  0.0 48.7 jit_solution(13611985889968134510)
XLA Ops:
  0.6 45.6 %modes_exchange_lags.1 = f32[16,128]{1,0:T(8,128)} custom-call(bf16[3,128,128,128]{3,2,1,0:T(8,128)(2,1)} %bitcast.6, s32[16,128]{1,0:T(8,128)} %bitcast.7, bf16[144,128]{1,0:T(8,128)(2,1)} %constant.8.clone.ty_hbm, bf16[2,288,128]{2,1,0:T(8,128)(2,1)} %constant.9.clone.tx_hbm, f32[65,16,128]{2,1,0:T(8,128)} %constant.10.clone.tz_hbm), custom_call_target="tpu_custom_call" | custom-call | tf_op jit(solution)/shard_map/modes_exchange_lags/pallas_call | solution.py:312
  46.2 1.2 %add_bitcast_fusion = (f32[128]{0:T(128)S(1)}, f32[1,128]{1,0:T(1,128)}) fusion(f32[16,128]{1,0:T(8,128)} %modes_exchange_lags.1), kind=kLoop, calls=%fused_computation.1 | loop fusion | flops 128 | bytes 1536 | tf_op jit(solution)/shard_map/div | solution.py:341
  47.4 1.3 %divide_bitcast_fusion = f32[1,16,128]{2,1,0:T(8,128)} fusion(f32[16,128]{1,0:T(8,128)} %modes_exchange_lags.1, f32[128]{0:T(128)S(1)} %get-tuple-element.2), kind=kLoop, calls=%fused_computation | loop fusion | flops 2048 | bytes 16896 | tf_op jit(solution)/shard_map/broadcast_in_dim | solution.py:341

commit v3 on v2

--- a/solution.py
+++ b/solution.py
@@ -80,7 +80,7 @@
     send_sem, late_sem, recv_sem,
 ):
     comps, grid_len, _, _ = frame_hbm.shape
-    chunk = 16
+    chunk = grid_len // data_sem.shape[1]
     chunks = grid_len // chunk
     me = lax.axis_index("frames")
     block = lax.axis_index("tblk")
@@ -104,8 +104,8 @@
     for comp in range(comps):
         for part in range(chunks):
             fetch(comp, part).start()
-        if comp == 0:
-            tx_in.start()
+            if comp == 0 and part == 0:
+                tx_in.start()
     tz_in.start()
 
     def greet(frame, in_block):
@@ -134,9 +134,11 @@
     freq_out.start()
 
     ty_in.wait()
+    tx_in.wait()
     table_y = ty_ref[...]
-    for comp in range(comps):
-
+
+    @pl.loop(0, comps)
+    def _(comp):
         @pl.loop(0, chunks)
         def _(part):
             fetch(comp, part).wait()
@@ -150,12 +152,7 @@
                 second = pl.multiple_of((x_at + 1) * 2 * PITCH, 8)
                 along_y[pl.ds(second, 2 * PITCH), :] = res[:, LANES:]
 
-        if comp == 0:
-            tx_in.wait()
-
-        @pl.loop(0, (HALF + 1) // 2)
-        def _(pair_at):
-            ky = pair_at * 2
+        for ky in range(0, HALF, 2):
 
             def take(row):
                 return along_y[pl.ds(row, grid_len, stride=2 * PITCH), :]
@@ -220,10 +217,7 @@
     used = (row & 3) != 3
     scale = f32(float(grid_len) ** -1.5)
 
-    @pl.loop(0, frames)
-    def _(step):
-        owner = lax.rem(me + step, frames)
-
+    def picked(owner):
         def leaf(mode):
             place = place_smem[owner, mode] * (2 * CHANNELS)
             freq = freq_smem[owner, mode]
@@ -248,20 +242,29 @@
         real_dot = jnp.sum(jnp.where(upper, along, f32(0)), axis=0, keepdims=True)
         imag_dot = jnp.sum(jnp.where(upper, f32(0), along), axis=0, keepdims=True)
         removed = wave * (jnp.where(upper, real_dot, imag_dot) / wave_sq)
-        transverse = current - jnp.where(used, removed, f32(0))
-        packet[owner] = transverse
+        return current - jnp.where(used, removed, f32(0))
+
+    @pl.loop(0, frames, step=2)
+    def _(step):
+        pair = [lax.rem(me + step + which, frames) for which in range(2)]
+        transverse = [picked(owner) for owner in pair]
+        for owner, value in zip(pair, transverse):
+            packet[owner] = value
 
         @pl.when(sends_back)
         def _():
-            backward(owner).start()
+            for owner in pair:
+                backward(owner).start()
 
         @pl.when(step > 0)
         def _():
-            within(owner).start()
+            within(pair[0]).start()
+
+        within(pair[1]).start()
 
         @pl.when(step == 0)
         def _():
-            held[me] = transverse
+            held[me] = transverse[0]
 
     @pl.when(jnp.logical_not(has_later))
     def _():
@@ -298,6 +301,16 @@
         @pl.loop(0, frames)
         def _(owner):
             backward(owner).wait_send()
+
+
+def finish_kernel(lagged_hbm, corr_ref, strength_ref, lagged_ref, sem):
+    lagged_in = pltpu.make_async_copy(lagged_hbm, lagged_ref, sem)
+    lagged_in.start()
+    lagged_in.wait()
+    lagged = lagged_ref[...]
+    strength = lagged[:1]
+    strength_ref[...] = strength
+    corr_ref[0] = lagged / (strength + f32(1e-06))
 
 
 def on_device(momentum, mode_list):
@@ -325,7 +338,7 @@
         + [
             pltpu.VMEM((frames, CHANNELS, LANES), f32),
             pltpu.VMEM((frames + lags, CHANNELS, LANES), f32),
-            pltpu.SemaphoreType.DMA((comps, grid_len // 16)),
+            pltpu.SemaphoreType.DMA((comps, 4)),
             pltpu.SemaphoreType.DMA((4,)),
             pltpu.SemaphoreType.DMA((2,)),
             pltpu.SemaphoreType.DMA((frames,)),
@@ -337,8 +350,17 @@
         ),
         name="modes_exchange_lags",
     )(frame, mode_rows, *[jnp.asarray(table) for table in tables])
-    strength = lagged[0:1]
-    return (lagged / (strength + 1e-06))[None], strength
+    return pl.pallas_call(
+        finish_kernel,
+        out_shape=(
+            jax.ShapeDtypeStruct((1, lags, LANES), f32),
+            jax.ShapeDtypeStruct((1, LANES), f32),
+        ),
+        in_specs=[pl.BlockSpec(memory_space=pl.ANY)],
+        scratch_shapes=[pltpu.VMEM(lagged.shape, f32), pltpu.SemaphoreType.DMA],
+        compiler_params=pltpu.CompilerParams(vmem_limit_bytes=56 * 1024 * 1024),
+        name="correlation",
+    )(lagged)
 
 
 def solution(mesh):

time: 49.1 us -> 35.3 us (0.72)
  Pallas kernels: 45.6 us -> 34.5 us
  other arithmetic: 2.49 us -> 0 us
    pallas_call x1, Pallas kernels: 45.6 us -> 33.2 us  [on_device(): pl.pallas_call(functools.partial(program_kernel, frames, blocks, lags), o...]
    pallas_call x0 -> x1, Pallas kernels: none -> 1.32 us  [on_device(): pl.pallas_call(finish_kernel, out_shape=(jax.ShapeDtypeStruct((1, lags, L...]
    broadcast_in_dim x1 -> x0, other arithmetic: 1.3 us -> none  [on_device(): return ((lagged / (strength + 1e-06))[None], strength)]
    div x1 -> x0, other arithmetic: 1.18 us -> none  [on_device(): return ((lagged / (strength + 1e-06))[None], strength)]
where the time goes in v3:
time: 35.3 us; the launch traced here: 35.1 us
  Pallas kernels  34.5 us (98%)
  between operations  0.64 us (2%)
    pallas_call x1, Pallas kernels, on_device(): pl.pallas_call(functools.partial(program_kernel, frames, blocks, lags), o...  33.2 us
    pallas_call x1, Pallas kernels, on_device(): pl.pallas_call(finish_kernel, out_shape=(jax.ShapeDtypeStruct((1, lags, L...  1.32 us

profile of v3, /device:TPU:0, one launch (start us, length us, event | category | flops | bytes accessed | tf_op | source)
XLA Modules:
  0.0 35.1 jit_solution(13766389784858365612)
XLA Ops:
  0.6 33.2 %modes_exchange_lags.1.lagged_hbm = f32[16,128]{1,0:T(8,128)} custom-call(bf16[3,128,128,128]{3,2,1,0:T(8,128)(2,1)} %bitcast.2, s32[16,128]{1,0:T(8,128)} %bitcast.3, bf16[144,128]{1,0:T(8,128)(2,1)} %constant.6.clone.ty_hbm, bf16[2,288,128]{2,1,0:T(8,128)(2,1)} %constant.7.clone.tx_hbm, f32[65,16,128]{2,1,0:T(8,128)} %constant.8.clone.tz_hbm), custom_call_target="tpu_custom_call" | custom-call | tf_op jit(solution)/shard_map/modes_exchange_lags/pallas_call | solution.py:325
  33.8 1.3 %correlation.1 = (f32[1,16,128]{2,1,0:T(8,128)}, f32[1,128]{1,0:T(1,128)}) custom-call(f32[16,128]{1,0:T(8,128)} %modes_exchange_lags.1.lagged_hbm), custom_call_target="tpu_custom_call" | custom-call | tf_op jit(solution)/shard_map/correlation/pallas_call | solution.py:353

commit v4 on v3

--- a/solution.py
+++ b/solution.py
@@ -1,4 +1,5 @@
 import functools
+import math
 
 import jax
 import jax.numpy as jnp
@@ -137,42 +138,54 @@
     tx_in.wait()
     table_y = ty_ref[...]
 
-    @pl.loop(0, comps)
-    def _(comp):
-        @pl.loop(0, chunks)
-        def _(part):
-            fetch(comp, part).wait()
-            for step in range(0, chunk, 2):
-                x_at = part * chunk + step
-                both = jnp.concatenate([data[comp, x_at], data[comp, x_at + 1]], axis=1)
-                res = jnp.dot(table_y, both, preferred_element_type=f32)
-                res = res[: 2 * PITCH] + res[2 * PITCH :]
-                first = pl.multiple_of(x_at * 2 * PITCH, 8)
-                along_y[pl.ds(first, 2 * PITCH), :] = res[:, :LANES]
-                second = pl.multiple_of((x_at + 1) * 2 * PITCH, 8)
-                along_y[pl.ds(second, 2 * PITCH), :] = res[:, LANES:]
-
-        for ky in range(0, HALF, 2):
-
-            def take(row):
-                return along_y[pl.ds(row, grid_len, stride=2 * PITCH), :]
-
-            cos_part = jnp.concatenate([take(ky), take(ky + 1)], axis=1)
-            sin_part = jnp.concatenate([take(PITCH + ky), take(PITCH + ky + 1)], axis=1)
-            values = jnp.concatenate([cos_part, sin_part], axis=0)
-            high = values.astype(bf16)
-            low = (values - high.astype(f32)).astype(bf16)
-            table_x = jnp.concatenate([tx_ref[0], tx_ref[1]], axis=1)
-            res = jnp.dot(table_x, high, preferred_element_type=f32)
-            res_low = jnp.dot(table_x[: 2 * ROWS], low, preferred_element_type=f32)
-            res = res[: 2 * ROWS] + res[2 * ROWS :] + res_low
-            half = CHANNELS // 2
-            for which in range(2):
-                lanes = slice(which * LANES, (which + 1) * LANES)
-                base = (ky + which) * ROWS * 2 * CHANNELS + comp
-                real, imag = res[:ROWS, lanes], res[ROWS:, lanes]
-                for at, value in enumerate((real, imag, imag, real)):
-                    plane[pl.ds(base + at * half, ROWS, stride=2 * CHANNELS), :] = value
+    def y_stage(comp, x_at):
+        both = jnp.concatenate([data[comp, x_at], data[comp, x_at + 1]], axis=1)
+        res = jnp.dot(table_y, both, preferred_element_type=f32)
+        res = res[: 2 * PITCH] + res[2 * PITCH :]
+        for which in range(2):
+            first = (x_at + which) * 2 * PITCH
+            lanes = slice(which * LANES, (which + 1) * LANES)
+            along_y[comp % 2, pl.ds(first, 2 * PITCH), :] = res[:, lanes]
+
+    def x_stage(comp, ky):
+        def take(row):
+            return along_y[comp % 2, pl.ds(row, grid_len, stride=2 * PITCH), :]
+
+        cos_part = jnp.concatenate([take(ky), take(ky + 1)], axis=1)
+        sin_part = jnp.concatenate([take(PITCH + ky), take(PITCH + ky + 1)], axis=1)
+        values = jnp.concatenate([cos_part, sin_part], axis=0)
+        high = values.astype(bf16)
+        low = (values - high.astype(f32)).astype(bf16)
+        table_x = jnp.concatenate([tx_ref[0], tx_ref[1]], axis=1)
+        res = jnp.dot(table_x, high, preferred_element_type=f32)
+        res_low = jnp.dot(table_x[: 2 * ROWS], low, preferred_element_type=f32)
+        res = res[: 2 * ROWS] + res[2 * ROWS :] + res_low
+        half = CHANNELS // 2
+        for which in range(2):
+            lanes = slice(which * LANES, (which + 1) * LANES)
+            base = (ky + which) * ROWS * 2 * CHANNELS + comp
+            real, imag = res[:ROWS, lanes], res[ROWS:, lanes]
+            for at, value in enumerate((real, imag, imag, real)):
+                plane[pl.ds(base + at * half, ROWS, stride=2 * CHANNELS), :] = value
+
+    x_pairs = list(range(0, grid_len, 2))
+    ky_pairs = list(range(0, HALF, 2))
+    for part in range(chunks):
+        fetch(0, part).wait()
+        for x_at in range(part * chunk, (part + 1) * chunk, 2):
+            y_stage(0, x_at)
+    for comp in range(comps):
+        ahead = x_pairs if comp + 1 < comps else []
+        if ahead:
+            for part in range(chunks):
+                fetch(comp + 1, part).wait()
+        done = 0
+        for count, ky in enumerate(ky_pairs):
+            x_stage(comp, ky)
+            until = len(ahead) * (count + 1) // len(ky_pairs)
+            for x_at in ahead[done:until]:
+                y_stage(comp + 1, x_at)
+            done = until
 
     place_out.wait()
     freq_out.wait()
@@ -244,23 +257,26 @@
         removed = wave * (jnp.where(upper, real_dot, imag_dot) / wave_sq)
         return current - jnp.where(used, removed, f32(0))
 
-    @pl.loop(0, frames, step=2)
+    group = math.gcd(frames, 4)
+
+    @pl.loop(0, frames, step=group)
     def _(step):
-        pair = [lax.rem(me + step + which, frames) for which in range(2)]
-        transverse = [picked(owner) for owner in pair]
-        for owner, value in zip(pair, transverse):
+        picks = [lax.rem(me + step + which, frames) for which in range(group)]
+        transverse = [picked(owner) for owner in picks]
+        for owner, value in zip(picks, transverse):
             packet[owner] = value
 
         @pl.when(sends_back)
         def _():
-            for owner in pair:
+            for owner in picks:
                 backward(owner).start()
 
         @pl.when(step > 0)
         def _():
-            within(pair[0]).start()
-
-        within(pair[1]).start()
+            within(picks[0]).start()
+
+        for owner in picks[1:]:
+            within(owner).start()
 
         @pl.when(step == 0)
         def _():
@@ -284,13 +300,19 @@
 
     anchors = held[pl.ds(0, frames)]
 
-    @pl.loop(0, lags)
-    def _(tau):
-        products = jnp.sum(anchors * held[pl.ds(tau, frames)], axis=0)
-        total = jnp.sum(products, axis=0, keepdims=True)
-        whole = f32(frames)
-        pairs = jnp.where(has_later, whole, whole - tau.astype(f32))
-        lagged_ref[pl.ds(tau, 1), :] = total / pairs
+    def lag_rows(first):
+        for tau in range(8):
+            products = jnp.sum(anchors * held[pl.ds(first + tau, frames)], axis=0)
+            total = jnp.sum(products, axis=0, keepdims=True)
+            lagged_ref[pl.ds(first + tau, 1), :] = total
+        taus = lax.broadcasted_iota(jnp.int32, (8, LANES), 0) + first
+        pairs = jnp.where(has_later, frames, frames - taus).astype(f32)
+        rows = pl.ds(first, 8)
+        lagged_ref[rows, :] = lagged_ref[rows, :] / pairs
+
+    @pl.loop(0, lags, step=8)
+    def _(first):
+        lag_rows(pl.multiple_of(first, 8))
 
     @pl.loop(1, frames)
     def _(step):
@@ -330,7 +352,7 @@
         scratch_shapes=[pltpu.VMEM(frame.shape, bf16), pltpu.VMEM(mode_rows.shape, jnp.int32)]
         + [pltpu.VMEM(table.shape, table.dtype) for table in tables]
         + [
-            pltpu.VMEM((grid_len * 2 * PITCH, LANES), f32),
+            pltpu.VMEM((2, grid_len * 2 * PITCH, LANES), f32),
             pltpu.VMEM(((HALF + 1) * ROWS * 2 * CHANNELS, LANES), f32),
         ]
         + places

time: 35.3 us -> 40.3 us (1.14)
  Pallas kernels: 34.5 us -> 39.5 us
    pallas_call x1, Pallas kernels: 33.2 us -> 38.1 us  [on_device(): pl.pallas_call(functools.partial(program_kernel, frames, blocks, lags), o...]
where the time goes in v4:
time: 40.3 us; the launch traced here: 40.1 us
  Pallas kernels  39.5 us (98%)
  between operations  0.64 us (2%)
    pallas_call x1, Pallas kernels, on_device(): pl.pallas_call(functools.partial(program_kernel, frames, blocks, lags), o...  38.1 us
    pallas_call x1, Pallas kernels, on_device(): pl.pallas_call(finish_kernel, out_shape=(jax.ShapeDtypeStruct((1, lags, L...  1.32 us

profile of v4, /device:TPU:0, one launch (start us, length us, event | category | flops | bytes accessed | tf_op | source)
XLA Modules:
  0.0 40.1 jit_solution(802915377744013877)
XLA Ops:
  0.6 38.1 %modes_exchange_lags.1.lagged_hbm = f32[16,128]{1,0:T(8,128)} custom-call(bf16[3,128,128,128]{3,2,1,0:T(8,128)(2,1)} %bitcast.2, s32[16,128]{1,0:T(8,128)} %bitcast.3, bf16[144,128]{1,0:T(8,128)(2,1)} %constant.6.clone.ty_hbm, bf16[2,288,128]{2,1,0:T(8,128)(2,1)} %constant.7.clone.tx_hbm, f32[65,16,128]{2,1,0:T(8,128)} %constant.8.clone.tz_hbm), custom_call_target="tpu_custom_call" | custom-call | tf_op jit(solution)/shard_map/modes_exchange_lags/pallas_call | solution.py:347
  38.8 1.3 %correlation.1 = (f32[1,16,128]{2,1,0:T(8,128)}, f32[1,128]{1,0:T(1,128)}) custom-call(f32[16,128]{1,0:T(8,128)} %modes_exchange_lags.1.lagged_hbm), custom_call_target="tpu_custom_call" | custom-call | tf_op jit(solution)/shard_map/correlation/pallas_call | solution.py:375

commit v5 on v3

--- a/solution.py
+++ b/solution.py
@@ -169,10 +169,10 @@
             half = CHANNELS // 2
             for which in range(2):
                 lanes = slice(which * LANES, (which + 1) * LANES)
-                base = (ky + which) * ROWS * 2 * CHANNELS + comp
+                base = (ky + which) * ROWS * CHANNELS + comp
                 real, imag = res[:ROWS, lanes], res[ROWS:, lanes]
-                for at, value in enumerate((real, imag, imag, real)):
-                    plane[pl.ds(base + at * half, ROWS, stride=2 * CHANNELS), :] = value
+                for at, value in enumerate((real, imag)):
+                    plane[pl.ds(base + at * half, ROWS, stride=CHANNELS), :] = value
 
     place_out.wait()
     freq_out.wait()
@@ -219,10 +219,11 @@
 
     def picked(owner):
         def leaf(mode):
-            place = place_smem[owner, mode] * (2 * CHANNELS)
+            place = place_smem[owner, mode] * CHANNELS
             freq = freq_smem[owner, mode]
-            value = plane[pl.ds(place, 2 * CHANNELS), :] * tz_ref[freq]
-            return value[:CHANNELS] + value[CHANNELS:]
+            value = plane[pl.ds(place, CHANNELS), :]
+            swapped = pltpu.roll(value, CHANNELS // 2, 0)
+            return value * tz_ref[freq, :CHANNELS] + swapped * tz_ref[freq, CHANNELS:]
 
         def tree(start, level):
             if level < 0:
@@ -284,13 +285,19 @@
 
     anchors = held[pl.ds(0, frames)]
 
-    @pl.loop(0, lags)
-    def _(tau):
-        products = jnp.sum(anchors * held[pl.ds(tau, frames)], axis=0)
-        total = jnp.sum(products, axis=0, keepdims=True)
-        whole = f32(frames)
-        pairs = jnp.where(has_later, whole, whole - tau.astype(f32))
-        lagged_ref[pl.ds(tau, 1), :] = total / pairs
+    def lag_rows(first):
+        for tau in range(8):
+            products = jnp.sum(anchors * held[pl.ds(first + tau, frames)], axis=0)
+            total = jnp.sum(products, axis=0, keepdims=True)
+            lagged_ref[pl.ds(first + tau, 1), :] = total
+        taus = lax.broadcasted_iota(jnp.int32, (8, LANES), 0) + first
+        pairs = jnp.where(has_later, frames, frames - taus).astype(f32)
+        rows = pl.ds(first, 8)
+        lagged_ref[rows, :] = lagged_ref[rows, :] / pairs
+
+    @pl.loop(0, lags, step=8)
+    def _(first):
+        lag_rows(pl.multiple_of(first, 8))
 
     @pl.loop(1, frames)
     def _(step):
@@ -331,7 +338,7 @@
         + [pltpu.VMEM(table.shape, table.dtype) for table in tables]
         + [
             pltpu.VMEM((grid_len * 2 * PITCH, LANES), f32),
-            pltpu.VMEM(((HALF + 1) * ROWS * 2 * CHANNELS, LANES), f32),
+            pltpu.VMEM(((HALF + 1) * ROWS * CHANNELS, LANES), f32),
         ]
         + places
         + places

time: 35.3 us -> 32.1 us (0.909)
  Pallas kernels: 34.5 us -> 31.2 us
    pallas_call x1, Pallas kernels: 33.2 us -> 29.9 us  [on_device(): pl.pallas_call(functools.partial(program_kernel, frames, blocks, lags), o...]
where the time goes in v5:
time: 32.1 us; the launch traced here: 31.9 us
  Pallas kernels  31.2 us (97%)
  between operations  0.64 us (2%)
    pallas_call x1, Pallas kernels, on_device(): pl.pallas_call(functools.partial(program_kernel, frames, blocks, lags), o...  29.9 us
    pallas_call x1, Pallas kernels, on_device(): pl.pallas_call(finish_kernel, out_shape=(jax.ShapeDtypeStruct((1, lags, L...  1.32 us

profile of v5, /device:TPU:0, one launch (start us, length us, event | category | flops | bytes accessed | tf_op | source)
XLA Modules:
  0.0 31.9 jit_solution(6236716542805263146)
XLA Ops:
  0.6 29.9 %modes_exchange_lags.1.lagged_hbm = f32[16,128]{1,0:T(8,128)} custom-call(bf16[3,128,128,128]{3,2,1,0:T(8,128)(2,1)} %bitcast.2, s32[16,128]{1,0:T(8,128)} %bitcast.3, bf16[144,128]{1,0:T(8,128)(2,1)} %constant.6.clone.ty_hbm, bf16[2,288,128]{2,1,0:T(8,128)(2,1)} %constant.7.clone.tx_hbm, f32[65,16,128]{2,1,0:T(8,128)} %constant.8.clone.tz_hbm), custom_call_target="tpu_custom_call" | custom-call | tf_op jit(solution)/shard_map/modes_exchange_lags/pallas_call | solution.py:332
  30.6 1.3 %correlation.1 = (f32[1,16,128]{2,1,0:T(8,128)}, f32[1,128]{1,0:T(1,128)}) custom-call(f32[16,128]{1,0:T(8,128)} %modes_exchange_lags.1.lagged_hbm), custom_call_target="tpu_custom_call" | custom-call | tf_op jit(solution)/shard_map/correlation/pallas_call | solution.py:360

commit v6 on v5

--- a/solution.py
+++ b/solution.py
@@ -245,9 +245,9 @@
         removed = wave * (jnp.where(upper, real_dot, imag_dot) / wave_sq)
         return current - jnp.where(used, removed, f32(0))
 
-    @pl.loop(0, frames, step=2)
+    @pl.loop(0, frames)
     def _(step):
-        pair = [lax.rem(me + step + which, frames) for which in range(2)]
+        pair = [lax.rem(me + step, frames)]
         transverse = [picked(owner) for owner in pair]
         for owner, value in zip(pair, transverse):
             packet[owner] = value
@@ -260,8 +260,6 @@
         @pl.when(step > 0)
         def _():
             within(pair[0]).start()
-
-        within(pair[1]).start()
 
         @pl.when(step == 0)
         def _():

time: 32.1 us -> 35.2 us (1.097)
  Pallas kernels: 31.2 us -> 34.2 us
    pallas_call x1, Pallas kernels: 29.9 us -> 32.9 us  [on_device(): pl.pallas_call(functools.partial(program_kernel, frames, blocks, lags), o...]
where the time goes in v6:
time: 35.2 us; the launch traced here: 34.9 us
  Pallas kernels  34.2 us (97%)
  between operations  0.64 us (2%)
    pallas_call x1, Pallas kernels, on_device(): pl.pallas_call(functools.partial(program_kernel, frames, blocks, lags), o...  32.9 us
    pallas_call x1, Pallas kernels, on_device(): pl.pallas_call(finish_kernel, out_shape=(jax.ShapeDtypeStruct((1, lags, L...  1.32 us

profile of v6, /device:TPU:0, one launch (start us, length us, event | category | flops | bytes accessed | tf_op | source)
XLA Modules:
  0.0 34.9 jit_solution(14164158361918267561)
XLA Ops:
  0.6 32.9 %modes_exchange_lags.1.lagged_hbm = f32[16,128]{1,0:T(8,128)} custom-call(bf16[3,128,128,128]{3,2,1,0:T(8,128)(2,1)} %bitcast.2, s32[16,128]{1,0:T(8,128)} %bitcast.3, bf16[144,128]{1,0:T(8,128)(2,1)} %constant.6.clone.ty_hbm, bf16[2,288,128]{2,1,0:T(8,128)(2,1)} %constant.7.clone.tx_hbm, f32[65,16,128]{2,1,0:T(8,128)} %constant.8.clone.tz_hbm), custom_call_target="tpu_custom_call" | custom-call | tf_op jit(solution)/shard_map/modes_exchange_lags/pallas_call | solution.py:330
  33.6 1.3 %correlation.1 = (f32[1,16,128]{2,1,0:T(8,128)}, f32[1,128]{1,0:T(1,128)}) custom-call(f32[16,128]{1,0:T(8,128)} %modes_exchange_lags.1.lagged_hbm), custom_call_target="tpu_custom_call" | custom-call | tf_op jit(solution)/shard_map/correlation/pallas_call | solution.py:358
